TPU v7x, 32 devices: a whole 2x2x4 slice. The times are simulated.
32 devices in a mesh: rows: 16 (over z, x, core), samp: 2 (over y).
Axes of the slice: x: 2, y: 2, z: 4, core: 2. Of those that a mesh axis runs over, the one named last changes fastest.
Arguments:
- sketch: float32 [256, 49152], P('samp', 'rows'), may hold values from -6 to 6
- probes: float32 [256, 49152], P('samp', 'rows'), may hold values from -6 to 6
- test_leaf: float32 [64, 256], replicated, may hold values from -0.375 to 0.375
- test_parent: float32 [64, 256], replicated, may hold values from -0.375 to 0.375
- leaf_far: int32 [192, 8], P(('rows', 'samp')), may hold values from 0 to 191, as said below
- leaf_count: int32 [192], P(('rows', 'samp')), may hold values from 1 to 8
- parent_far: int32 [96, 8], P(('rows', 'samp')), may hold values from 0 to 95, as said below
- parent_count: int32 [96], P(('rows', 'samp')), may hold values from 1 to 8
Outputs:
- leaf_basis: float32 [64, 49152], P(None, ('rows', 'samp'))
- leaf_coupling: float32 [192, 8, 4096], P(('rows', 'samp'))
- transfer: float32 [96, 64, 128], P(('rows', 'samp'))
- parent_coupling: float32 [96, 8, 4096], P(('rows', 'samp'))
Inputs may be any that keep to these rules, and one draw needn't show every extreme that they name: leaf_far[i, k] = j satisfies 2 <= |i - j| <= 6. `parent_far`: with b(p) = p // 3, a partner q of p has b(q) - b(p) a nonzero multiple of 2, at most 4 * 2 in magnitude.
All inputs are finite; a program needn't handle non-finite values.
Results may differ from a plain program's by a relative error of at most 0.0041.
Values may be sent and summed in bfloat16 or wider, within the bound.
A program may use at most 64 MiB of HBM per device.

v0:
```python
import functools

import jax
import jax.numpy as jnp
from jax import lax
from jax.experimental import pallas as pl
from jax.experimental.pallas import tpu as pltpu
from jax.sharding import PartitionSpec as P

LEAF = 256
REACH = 4
LANES = 128

F32 = jnp.float32
BF16 = jnp.bfloat16
MESH = pl.DeviceIdType.MESH
highest = lax.Precision.HIGHEST


def dot_nn(a, b, precision=None):
    return lax.dot_general(
        a, b, (((1,), (0,)), ((), ())), precision=precision, preferred_element_type=F32
    )


def dot_nt(a, b, precision=None):
    return lax.dot_general(
        a, b, (((1,), (1,)), ((), ())), precision=precision, preferred_element_type=F32
    )


def split(x):
    hi = x.astype(BF16)
    return hi, (x - hi.astype(F32)).astype(BF16)


def three_pass(dot, a, b):
    a_hi, a_lo = split(a)
    b_hi, b_lo = split(b)
    return dot(a_hi, b_hi) + (dot(a_lo, b_hi) + dot(a_hi, b_lo))


def row_of(x, s):
    return jnp.broadcast_to(x[s : s + 1, :], x.shape)


def inverse_factors(grams):
    rank = grams[0].shape[0]
    lane = lax.broadcasted_iota(jnp.int32, (8, LANES), 1)
    row = lax.broadcasted_iota(jnp.int32, (8, LANES), 0)
    within = lax.rem(lane, rank)
    base = lane - within
    blocks = rank // 8
    results = []
    pairs = [(grams[i], grams[min(i + 1, len(grams) - 1)]) for i in range(0, len(grams), 2)]
    states = []
    for left, right in pairs:
        whole = jnp.concatenate([left, right], axis=1)
        states.append([whole[8 * t : 8 * t + 8, :] for t in range(blocks)])
    scales = [[None] * blocks for _ in pairs]
    for b in range(blocks):
        in_block = (within >= 8 * b) & (within < 8 * b + 8)
        for at, tiles in enumerate(states):
            tile = tiles[b]
            cols = [
                jnp.take_along_axis(tile, base + (8 * b + j), axis=1, mode="promise_in_bounds")
                for j in range(8)
            ]
            scale = jnp.zeros((8, LANES), F32)
            inv_pivots, heads, pivot_rows = [], [], []
            for s in range(8):
                pivot = row_of(cols[s], s)
                inv_pivot = 1.0 / pivot
                scale = jnp.where(row == s, lax.rsqrt(pivot), scale)
                f = jnp.where(row > s, cols[s] * inv_pivot, 0.0)
                head = [None] * 8
                for j in range(s + 1, 8):
                    head[j] = row_of(cols[j], s)
                    cols[j] = cols[j] - f * head[j]
                here = within == 8 * b + s
                pivot_row = jnp.where(here, 1.0, row_of(tile, s))
                tile = jnp.where(here & (row > s), 0.0, tile) - f * pivot_row
                inv_pivots.append(inv_pivot)
                heads.append(head)
                pivot_rows.append(pivot_row)
            scales[at][b] = scale
            tiles[b] = tile
            for t in range(b + 1, blocks):
                tile = tiles[t]
                cols = [
                    jnp.take_along_axis(tile, base + (8 * b + j), axis=1, mode="promise_in_bounds")
                    for j in range(8)
                ]
                for s in range(8):
                    f = cols[s] * inv_pivots[s]
                    for j in range(s + 1, 8):
                        cols[j] = cols[j] - f * heads[s][j]
                    here = within == 8 * b + s
                    tile = jnp.where(here, 0.0, tile) - f * pivot_rows[s]
                tiles[t] = tile
    for at, tiles in enumerate(states):
        done = []
        for b in range(blocks):
            lower = jnp.where(within < row + 8 * b, tiles[b], 0.0)
            lower = jnp.where(within == row + 8 * b, 1.0, lower)
            done.append(lower * scales[at][b])
        whole = jnp.concatenate(done, axis=0)
        results += [whole[:, :rank], whole[:, rank : 2 * rank]]
    return results[: len(grams)]


def put_columns(ref, first, value):
    for c in range(value.shape[1] // LANES):
        ref[c, first : first + value.shape[0], :] = value[:, c * LANES : (c + 1) * LANES]


def even_then_odd(ref, first, rows):
    parts = [
        jnp.concatenate(
            [ref[c, pl.ds(first + o, rows // 2, stride=2), :] for o in (0, 1)], axis=0
        )
        for c in range(ref.shape[0])
    ]
    return jnp.concatenate(parts, axis=1)


def flatten_rows(ref, product, slot, slots):
    half = product.shape[0] // 2
    packed = jnp.concatenate([product[:half], product[half:]], axis=1)
    ref[pl.ds(slot, half, stride=slots), :] = packed


def kernel(
    sizes,
    leaf_far, leaf_count, parent_far, parent_count, test_leaf, test_parent, sketch, probes,
    basis_out, coupling_out, transfer_out, parent_out,
    raw, y_send, o_send, y_hi, y_lo, o_hi, o_lo, w_buf, w_cols, v_all, v_own, a_cols, b_all, flat,
    load_sem, y_sems, o_sems, v_sems, b_sems,
):
    n_rows, n_samp = sizes
    owned, slots = leaf_far.shape
    per_device = parent_far.shape[0]
    rank, samples = test_leaf.shape
    local = samples // n_samp
    width = owned * LEAF
    row, samp = lax.axis_index("rows"), lax.axis_index("samp")
    me = row * n_samp + samp
    last = n_rows * n_samp - 1
    shifts = [s for s in range(-REACH, REACH + 1) if s != 0]

    def at(linear):
        return (linear // n_samp, lax.rem(linear, n_samp))

    def others(act):
        for o in range(1, n_samp):
            act(row, lax.rem(samp + o, n_samp))

    def load(array, which, target):
        return pltpu.make_async_copy(
            array.at[:, pl.ds(pl.multiple_of(target * width, width), width)],
            raw.at[which, target],
            load_sem.at[which, target],
        )

    for which, array in ((0, sketch), (1, probes)):
        for o in range(n_samp):
            load(array, which, lax.rem(samp + 1 + o, n_samp)).start()

    barrier = pltpu.get_barrier_semaphore()

    peers = n_samp - 1
    for o in range(1, n_samp):
        pl.semaphore_signal(
            barrier, inc=1, device_id=(row, lax.rem(samp + o, n_samp)), device_id_type=MESH
        )
    met = [(at(me - 1), (samp == 0) & (row > 0))]
    met += [(at(me + 1), (samp == n_samp - 1) & (row < n_rows - 1))]
    met += [((row + s, samp), (row + s >= 0) & (row + s < n_rows)) for s in shifts]
    for device, valid in met:
        peers = peers + valid.astype(jnp.int32)

        @pl.when(valid)
        def _(device=device):
            pl.semaphore_signal(barrier, inc=1, device_id=device, device_id_type=MESH)

    def exchange(which, send, land, sems):
        def copy(o):
            target = lax.rem(samp + o, n_samp)
            return pltpu.make_async_remote_copy(
                src_ref=send.at[target],
                dst_ref=land.at[samp],
                send_sem=sems.at[0, o],
                recv_sem=sems.at[1, o],
                device_id=(row, target),
                device_id_type=MESH,
            )

        def arrival(o):
            source = lax.rem(samp + n_samp - o, n_samp)
            return pltpu.make_async_remote_copy(
                src_ref=send.at[source],
                dst_ref=land.at[source],
                send_sem=sems.at[0, o],
                recv_sem=sems.at[1, o],
                device_id=(row, source),
                device_id_type=MESH,
            )

        return copy, arrival

    def prepare(array, which, send):
        for o in range(1, n_samp):
            target = lax.rem(samp + o, n_samp)
            load(array, which, target).wait()
            send[target] = raw[which, target].astype(BF16)

    def prepare_own(array, which, hi_ref, lo_ref):
        load(array, which, samp).wait()
        lo_ref[...] = jnp.zeros_like(lo_ref)
        hi, lo = split(raw[which, samp])
        hi_ref[samp] = hi
        lo_ref[samp] = lo

    y_copy, y_arrival = exchange(0, y_send, y_hi, y_sems)
    o_copy, o_arrival = exchange(1, o_send, o_hi, o_sems)

    prepare(sketch, 0, y_send)
    pl.semaphore_wait(barrier, peers)

    for o in range(1, n_samp):
        y_copy(o).start()
    prepare_own(sketch, 0, y_hi, y_lo)
    prepare(probes, 1, o_send)
    prepare_own(probes, 1, o_hi, o_lo)
    for o in range(1, n_samp):
        y_copy(o).wait_send()
    for o in range(1, n_samp):
        o_copy(o).start()
    for o in range(1, n_samp):
        y_arrival(o).wait_recv()

    test_hi, test_lo = split(test_leaf[...])
    both = jnp.concatenate([test_hi, test_lo], axis=0)

    def leaf_columns(ref, i):
        return ref[:, :, i * LEAF : (i + 1) * LEAF].reshape(samples, LEAF)

    blocks, grams = [], []
    for i in range(owned):
        hi, lo = leaf_columns(y_hi, i), leaf_columns(y_lo, i)
        wide = dot_nn(both, hi)
        block = wide[:rank] + (wide[rank:] + dot_nn(test_hi, lo))
        blocks.append(block)
        grams.append(dot_nt(block, block, highest))
    inverses = inverse_factors(grams)
    bases = []
    for i in range(owned):
        basis = dot_nn(inverses[i], blocks[i], highest)
        basis_out[:, i * LEAF : (i + 1) * LEAF] = basis
        hi, lo = split(basis)
        bases.append((hi, jnp.concatenate([hi, lo], axis=0)))

    def project(i, hi_ref, lo_ref):
        hi, pair = bases[i]
        wide = dot_nt(pair, leaf_columns(hi_ref, i))
        return wide[:rank] + (wide[rank:] + dot_nt(hi, leaf_columns(lo_ref, i)))

    for i in range(owned):
        w = project(i, y_hi, y_lo)
        w_buf[i * rank : (i + 1) * rank, :] = w
        put_columns(w_cols, i * rank, w)

    test_coarse = test_parent[...]
    ranges, coarse_grams = [], []
    for p in range(per_device):
        c = dot_nt(test_coarse, w_buf[2 * p * rank : 2 * (p + 1) * rank, :], highest)
        ranges.append(c)
        coarse_grams.append(dot_nt(c, c, highest))

    for o in range(1, n_samp):
        o_copy(o).wait_send()
        o_arrival(o).wait_recv()
    for i in range(owned):
        v = project(i, o_hi, o_lo)
        v_own[i * rank : (i + 1) * rank, :] = v
        v_all[owned + i] = v.astype(BF16)

    def halo(step):
        side = 0 if step == 1 else 1
        return pltpu.make_async_remote_copy(
            src_ref=v_all.at[pl.ds(owned, owned)],
            dst_ref=v_all.at[pl.ds(0 if step == 1 else 2 * owned, owned)],
            send_sem=v_sems.at[0, side],
            recv_sem=v_sems.at[1, side],
            device_id=at(me + step),
            device_id_type=MESH,
        )

    def when(valid, act):
        @pl.when(valid)
        def _():
            act()

    when(me < last, lambda: halo(1).start())
    when(me > 0, lambda: halo(-1).start())

    coarse_inverses = inverse_factors(coarse_grams)
    transfers = []
    for p in range(per_device):
        t = dot_nn(coarse_inverses[p], ranges[p], highest)
        transfer_out[p] = t
        transfers.append(t)
        b = three_pass(dot_nn, t, v_own[2 * p * rank : 2 * (p + 1) * rank, :])
        b_all[REACH, p] = b.astype(BF16)

    def coarse(s):
        return pltpu.make_async_remote_copy(
            src_ref=b_all.at[REACH],
            dst_ref=b_all.at[REACH - s],
            send_sem=b_sems.at[0, REACH - s],
            recv_sem=b_sems.at[1, REACH - s],
            device_id=(row + s, samp),
            device_id_type=MESH,
        )

    def reaches(s):
        return (row + s >= 0) & (row + s < n_rows)

    for s in shifts:
        when(reaches(s), lambda s=s: coarse(s).start())

    for p in range(per_device):
        a = three_pass(dot_nn, transfers[p], w_buf[2 * p * rank : 2 * (p + 1) * rank, :])
        put_columns(a_cols, p * rank, a)

    when(me > 0, lambda: halo(1).wait_recv())
    when(me < last, lambda: halo(-1).wait_recv())
    half = rank // 2
    first_leaf = me * owned
    scale = 1.0 / samples
    for i in range(owned):
        hi, lo = split(even_then_odd(w_cols, i * rank, rank))
        lhs = jnp.concatenate([hi, lo], axis=0)
        for k in range(slots):
            v = v_all[jnp.clip(leaf_far[i, k] - first_leaf + owned, 0, 3 * owned - 1)]
            wide = dot_nt(lhs, v)
            used = jnp.where(k < leaf_count[i], scale, 0.0).astype(F32)
            flatten_rows(flat.at[i], (wide[:rank] + wide[rank:]) * used, k, slots)
        for m in range(half):
            coupling_out[i, :, m * LANES : (m + 1) * LANES] = flat[i, m * slots : (m + 1) * slots, :]

    for s in shifts:
        when(reaches(-s), lambda s=s: coarse(s).wait_recv())
    for p in range(per_device):
        lhs = even_then_odd(a_cols, p * rank, rank).astype(BF16)
        for k in range(slots):
            q = parent_far[p, k]
            from_here = q // (per_device * n_samp) - row + REACH
            b = b_all[jnp.clip(from_here, 0, 2 * REACH), lax.rem(q, per_device)]
            used = jnp.where(k < parent_count[p], scale, 0.0).astype(F32)
            flatten_rows(flat.at[owned + p], dot_nt(lhs, b) * used, k, slots)
        for m in range(half):
            parent_out[p, :, m * LANES : (m + 1) * LANES] = flat[
                owned + p, m * slots : (m + 1) * slots, :
            ]

    when(me < last, lambda: halo(1).wait_send())
    when(me > 0, lambda: halo(-1).wait_send())
    for s in shifts:
        when(reaches(s), lambda s=s: coarse(s).wait_send())


def solution(mesh):
    n_rows, n_samp = mesh.shape["rows"], mesh.shape["samp"]

    def body(sketch, probes, test_leaf, test_parent, leaf_far, leaf_count, parent_far, parent_count):
        rank, samples = test_leaf.shape
        owned, slots = leaf_far.shape
        per_device = parent_far.shape[0]
        local = samples // n_samp
        width = owned * LEAF
        vmem = pl.BlockSpec(memory_space=pltpu.VMEM)
        smem = pl.BlockSpec(memory_space=pltpu.SMEM)
        hbm = pl.BlockSpec(memory_space=pl.ANY)
        blocks = (n_samp, local, width)
        return pl.pallas_call(
            functools.partial(kernel, (n_rows, n_samp)),
            out_shape=(
                jax.ShapeDtypeStruct((rank, width), F32),
                jax.ShapeDtypeStruct((owned, slots, rank * rank), F32),
                jax.ShapeDtypeStruct((per_device, rank, 2 * rank), F32),
                jax.ShapeDtypeStruct((per_device, slots, rank * rank), F32),
            ),
            in_specs=[smem] * 4 + [vmem] * 2 + [hbm] * 2,
            out_specs=(vmem,) * 4,
            scratch_shapes=[
                pltpu.VMEM((2,) + blocks, F32),
                pltpu.VMEM(blocks, BF16),
                pltpu.VMEM(blocks, BF16),
                pltpu.VMEM(blocks, BF16),
                pltpu.VMEM(blocks, BF16),
                pltpu.VMEM(blocks, BF16),
                pltpu.VMEM(blocks, BF16),
                pltpu.VMEM((owned * rank, samples), F32),
                pltpu.VMEM((samples // LANES, owned * rank, LANES), F32),
                pltpu.VMEM((3 * owned, rank, samples), BF16),
                pltpu.VMEM((owned * rank, samples), F32),
                pltpu.VMEM((samples // LANES, per_device * rank, LANES), F32),
                pltpu.VMEM((2 * REACH + 1, per_device, rank, samples), BF16),
                pltpu.VMEM((owned + per_device, slots * rank // 2, LANES), F32),
                pltpu.SemaphoreType.DMA((2, n_samp)),
                pltpu.SemaphoreType.DMA((2, n_samp)),
                pltpu.SemaphoreType.DMA((2, n_samp)),
                pltpu.SemaphoreType.DMA((2, 2)),
                pltpu.SemaphoreType.DMA((2, 2 * REACH + 1)),
            ],
            compiler_params=pltpu.CompilerParams(
                collective_id=0, has_side_effects=True, vmem_limit_bytes=40 * 1024 * 1024
            ),
            cost_estimate=pl.CostEstimate(
                flops=10**9, bytes_accessed=5 * 10**6, transcendentals=0
            ),
        )(leaf_far, leaf_count, parent_far, parent_count, test_leaf, test_parent, sketch, probes)

    return jax.shard_map(
        body,
        mesh=mesh,
        in_specs=(
            P("samp", "rows"),
            P("samp", "rows"),
            P(),
            P(),
            P(("rows", "samp"), None),
            P(("rows", "samp")),
            P(("rows", "samp"), None),
            P(("rows", "samp")),
        ),
        out_specs=(
            P(None, ("rows", "samp")),
            P(("rows", "samp"), None, None),
            P(("rows", "samp"), None, None),
            P(("rows", "samp"), None, None),
        ),
        check_vma=False,
    )
```

profile of v0, /device:TPU:9, one launch (start us, length us, event | category | flops | bytes accessed | tf_op | source)
XLA Modules:
  0.0 48.1 jit_solution(10685336448665549493)
XLA Ops:
  0.6 0.0 copy-start
  0.6 1.4 %copy-done = f32[128,3072]{1,0:T(8,128)S(1)} copy-done((f32[128,3072]{1,0:T(8,128)S(1)}, f32[128,3072]{1,0:T(8,128)}, u32[]{:S(2)}) %copy-start) | copy-done | bytes 1572888
  2.0 0.0 copy-start.1
  2.0 1.4 %copy-done.1 = f32[128,3072]{1,0:T(8,128)S(1)} copy-done((f32[128,3072]{1,0:T(8,128)S(1)}, f32[128,3072]{1,0:T(8,128)}, u32[]{:S(2)}) %copy-start.1) | copy-done | bytes 1572888
  3.5 0.0 copy-start.2
  3.5 0.8 %copy-done.2 = f32[64,256]{1,0:T(8,128)S(1)} copy-done((f32[64,256]{1,0:T(8,128)S(1)}, f32[64,256]{1,0:T(8,128)}, u32[]{:S(2)}) %copy-start.2) | copy-done | bytes 65560
  4.3 0.0 copy-start.3
  4.3 0.8 %copy-done.3 = f32[64,256]{1,0:T(8,128)S(1)} copy-done((f32[64,256]{1,0:T(8,128)S(1)}, f32[64,256]{1,0:T(8,128)}, u32[]{:S(2)}) %copy-start.3) | copy-done | bytes 65560
  5.1 0.0 copy-start.4
  5.1 0.7 %copy-done.4 = s32[6,8]{1,0:T(8,128)S(1)} copy-done((s32[6,8]{1,0:T(8,128)S(1)}, s32[6,8]{1,0:T(8,128)}, u32[]{:S(2)}) %copy-start.4) | copy-done | bytes 216
  5.8 0.0 copy-start.5
  5.8 0.7 %copy-done.5 = s32[3,8]{1,0:T(4,128)S(1)} copy-done((s32[3,8]{1,0:T(4,128)S(1)}, s32[3,8]{1,0:T(4,128)}, u32[]{:S(2)}) %copy-start.5) | copy-done | bytes 120
  6.5 0.0 copy-start.6
  6.5 0.7 %copy-done.6 = s32[6]{0:T(128)S(1)} copy-done((s32[6]{0:T(128)S(1)}, s32[6]{0:T(128)}, u32[]{:S(2)}) %copy-start.6) | copy-done | bytes 48
  7.2 0.0 copy-start.7
  7.2 0.7 %copy-done.7 = s32[3]{0:T(128)S(1)} copy-done((s32[3]{0:T(128)S(1)}, s32[3]{0:T(128)}, u32[]{:S(2)}) %copy-start.7) | copy-done | bytes 36
  7.8 37.2 %shard_map.111 = (f32[64,1536]{1,0:T(8,128)S(1)}, f32[6,8,4096]{2,1,0:T(8,128)S(1)}, f32[3,64,128]{2,1,0:T(8,128)S(1)}, f32[3,8,4096]{2,1,0:T(8,128)S(1)}) custom-call(s32[6,8]{1,0:T(8,128)S(1)} %copy-done.4, s32[6]{0:T(128)S(1)} %copy-done.6, s32[3,8]{1,0:T(4,128)S(1)} %copy-done.5, s32[3]{0:T(128)S(1)} %copy-done.7, f32[64,256]{1,0:T(8,128)S(1)} %copy-done.2, ...), custom_call_target="tpu_custom_call" | custom-call | flops 1000000000 | bytes 5000000 | tf_op jit(solution)/shard_map/pallas_call | solution.py:386
  45.0 0.7 %copy.16 = f32[64,1536]{1,0:T(8,128)} copy(f32[64,1536]{1,0:T(8,128)S(1)} %get-tuple-element.8) | data formatting | bytes 786432
  45.8 0.9 %copy.17 = f32[6,8,4096]{2,1,0:T(8,128)} copy(f32[6,8,4096]{2,1,0:T(8,128)S(1)} %get-tuple-element.9) | data formatting | bytes 1572864
  46.7 0.6 %copy.18 = f32[3,64,128]{2,1,0:T(8,128)} copy(f32[3,64,128]{2,1,0:T(8,128)S(1)} %get-tuple-element.10) | data formatting | bytes 196608
  47.3 0.7 %copy.19 = f32[3,8,4096]{2,1,0:T(8,128)} copy(f32[3,8,4096]{2,1,0:T(8,128)S(1)} %get-tuple-element.11) | data formatting | bytes 786432
Async XLA Ops:
  0.6 1.4 %copy-start = (f32[128,3072]{1,0:T(8,128)S(1)}, f32[128,3072]{1,0:T(8,128)}, u32[]{:S(2)}) copy-start(f32[128,3072]{1,0:T(8,128)} %sketch.1) | copy-start | bytes 4718596
  2.0 1.4 %copy-start.1 = (f32[128,3072]{1,0:T(8,128)S(1)}, f32[128,3072]{1,0:T(8,128)}, u32[]{:S(2)}) copy-start(f32[128,3072]{1,0:T(8,128)} %probes.1) | copy-start | bytes 4718596
  3.5 0.8 %copy-start.2 = (f32[64,256]{1,0:T(8,128)S(1)}, f32[64,256]{1,0:T(8,128)}, u32[]{:S(2)}) copy-start(f32[64,256]{1,0:T(8,128)} %test_leaf.1) | copy-start | bytes 196612
  4.3 0.8 %copy-start.3 = (f32[64,256]{1,0:T(8,128)S(1)}, f32[64,256]{1,0:T(8,128)}, u32[]{:S(2)}) copy-start(f32[64,256]{1,0:T(8,128)} %test_parent.1) | copy-start | bytes 196612
  5.1 0.7 %copy-start.4 = (s32[6,8]{1,0:T(8,128)S(1)}, s32[6,8]{1,0:T(8,128)}, u32[]{:S(2)}) copy-start(s32[6,8]{1,0:T(8,128)} %leaf_far.1) | copy-start | bytes 580
  5.8 0.7 %copy-start.5 = (s32[3,8]{1,0:T(4,128)S(1)}, s32[3,8]{1,0:T(4,128)}, u32[]{:S(2)}) copy-start(s32[3,8]{1,0:T(4,128)} %parent_far.1) | copy-start | bytes 292
  6.5 0.7 %copy-start.6 = (s32[6]{0:T(128)S(1)}, s32[6]{0:T(128)}, u32[]{:S(2)}) copy-start(s32[6]{0:T(128)} %leaf_count.1) | copy-start | bytes 76
  7.2 0.7 %copy-start.7 = (s32[3]{0:T(128)S(1)}, s32[3]{0:T(128)}, u32[]{:S(2)}) copy-start(s32[3]{0:T(128)} %parent_count.1) | copy-start | bytes 40
where the time goes:
time: 48.4 us; the launch traced here: 48.1 us
  Pallas kernels  37.2 us (77%)
  local copies, waits for them, and re-layouts  10.2 us (21%)
  between operations  0.66 us (1%)
    pallas_call x1, Pallas kernels, body(): pl.pallas_call(functools.partial(kernel, (n_rows, n_samp)), out_shape=(ja...  37.2 us
    unnamed x20, local copies, waits for them, and re-layouts  10.2 us

commit v1 on v0

--- a/solution.py
+++ b/solution.py
@@ -132,10 +132,11 @@
 
 def kernel(
     sizes,
-    leaf_far, leaf_count, parent_far, parent_count, test_leaf, test_parent, sketch, probes,
+    far_in, count_in, coarse_far_in, coarse_count_in, test_in, test_coarse_in, sketch, probes,
     basis_out, coupling_out, transfer_out, parent_out,
     raw, y_send, o_send, y_hi, y_lo, o_hi, o_lo, w_buf, w_cols, v_all, v_own, a_cols, b_all, flat,
-    load_sem, y_sems, o_sems, v_sems, b_sems,
+    leaf_far, leaf_count, parent_far, parent_count, test_leaf, test_parent,
+    load_sem, small_sem, y_sems, o_sems, v_sems, b_sems,
 ):
     n_rows, n_samp = sizes
     owned, slots = leaf_far.shape
@@ -166,6 +167,20 @@
         for o in range(n_samp):
             load(array, which, lax.rem(samp + 1 + o, n_samp)).start()
 
+    small = [
+        pltpu.make_async_copy(source, target, small_sem.at[i])
+        for i, (source, target) in enumerate((
+            (test_in, test_leaf),
+            (test_coarse_in, test_parent),
+            (far_in, leaf_far),
+            (count_in, leaf_count),
+            (coarse_far_in, parent_far),
+            (coarse_count_in, parent_count),
+        ))
+    ]
+    for copy in small:
+        copy.start()
+
     barrier = pltpu.get_barrier_semaphore()
 
     peers = n_samp - 1
@@ -238,6 +253,9 @@
         o_copy(o).start()
     for o in range(1, n_samp):
         y_arrival(o).wait_recv()
+
+    for copy in small:
+        copy.wait()
 
     test_hi, test_lo = split(test_leaf[...])
     both = jnp.concatenate([test_hi, test_lo], axis=0)
@@ -352,13 +370,15 @@
     for s in shifts:
         when(reaches(-s), lambda s=s: coarse(s).wait_recv())
     for p in range(per_device):
-        lhs = even_then_odd(a_cols, p * rank, rank).astype(BF16)
+        hi, lo = split(even_then_odd(a_cols, p * rank, rank))
+        lhs = jnp.concatenate([hi, lo], axis=0)
         for k in range(slots):
             q = parent_far[p, k]
             from_here = q // (per_device * n_samp) - row + REACH
             b = b_all[jnp.clip(from_here, 0, 2 * REACH), lax.rem(q, per_device)]
             used = jnp.where(k < parent_count[p], scale, 0.0).astype(F32)
-            flatten_rows(flat.at[owned + p], dot_nt(lhs, b) * used, k, slots)
+            wide = dot_nt(lhs, b)
+            flatten_rows(flat.at[owned + p], (wide[:rank] + wide[rank:]) * used, k, slots)
         for m in range(half):
             parent_out[p, :, m * LANES : (m + 1) * LANES] = flat[
                 owned + p, m * slots : (m + 1) * slots, :
@@ -368,6 +388,14 @@
     when(me > 0, lambda: halo(-1).wait_send())
     for s in shifts:
         when(reaches(s), lambda s=s: coarse(s).wait_send())
+
+
+def hand_over(*refs):
+    copies = [pltpu.make_async_copy(refs[i], refs[4 + i], refs[8].at[i]) for i in range(4)]
+    for copy in copies:
+        copy.start()
+    for copy in copies:
+        copy.wait()
 
 
 def solution(mesh):
@@ -380,10 +408,9 @@
         local = samples // n_samp
         width = owned * LEAF
         vmem = pl.BlockSpec(memory_space=pltpu.VMEM)
-        smem = pl.BlockSpec(memory_space=pltpu.SMEM)
-        hbm = pl.BlockSpec(memory_space=pl.ANY)
+        hbm = pl.BlockSpec(memory_space=pltpu.HBM)
         blocks = (n_samp, local, width)
-        return pl.pallas_call(
+        made = pl.pallas_call(
             functools.partial(kernel, (n_rows, n_samp)),
             out_shape=(
                 jax.ShapeDtypeStruct((rank, width), F32),
@@ -391,7 +418,7 @@
                 jax.ShapeDtypeStruct((per_device, rank, 2 * rank), F32),
                 jax.ShapeDtypeStruct((per_device, slots, rank * rank), F32),
             ),
-            in_specs=[smem] * 4 + [vmem] * 2 + [hbm] * 2,
+            in_specs=[hbm] * 8,
             out_specs=(vmem,) * 4,
             scratch_shapes=[
                 pltpu.VMEM((2,) + blocks, F32),
@@ -408,19 +435,34 @@
                 pltpu.VMEM((samples // LANES, per_device * rank, LANES), F32),
                 pltpu.VMEM((2 * REACH + 1, per_device, rank, samples), BF16),
                 pltpu.VMEM((owned + per_device, slots * rank // 2, LANES), F32),
+                pltpu.SMEM(leaf_far.shape, jnp.int32),
+                pltpu.SMEM(leaf_count.shape, jnp.int32),
+                pltpu.SMEM(parent_far.shape, jnp.int32),
+                pltpu.SMEM(parent_count.shape, jnp.int32),
+                pltpu.VMEM(test_leaf.shape, F32),
+                pltpu.VMEM(test_parent.shape, F32),
                 pltpu.SemaphoreType.DMA((2, n_samp)),
+                pltpu.SemaphoreType.DMA((6,)),
                 pltpu.SemaphoreType.DMA((2, n_samp)),
                 pltpu.SemaphoreType.DMA((2, n_samp)),
                 pltpu.SemaphoreType.DMA((2, 2)),
                 pltpu.SemaphoreType.DMA((2, 2 * REACH + 1)),
             ],
             compiler_params=pltpu.CompilerParams(
-                collective_id=0, has_side_effects=True, vmem_limit_bytes=40 * 1024 * 1024
+                collective_id=0, has_side_effects=True, vmem_limit_bytes=62 * 1024 * 1024
             ),
             cost_estimate=pl.CostEstimate(
                 flops=10**9, bytes_accessed=5 * 10**6, transcendentals=0
             ),
         )(leaf_far, leaf_count, parent_far, parent_count, test_leaf, test_parent, sketch, probes)
+        return pl.pallas_call(
+            hand_over,
+            out_shape=tuple(jax.ShapeDtypeStruct(x.shape, x.dtype) for x in made),
+            in_specs=[hbm] * 4,
+            out_specs=(hbm,) * 4,
+            scratch_shapes=[pltpu.SemaphoreType.DMA((4,))],
+            compiler_params=pltpu.CompilerParams(vmem_limit_bytes=62 * 1024 * 1024),
+        )(*made)
 
     return jax.shard_map(
         body,

time: 48.4 us -> 90.4 us (1.87)
  Pallas kernels: 37.2 us -> 89.6 us
  local copies, waits for them, and re-layouts: 10.2 us -> 0 us
    pallas_call x0 -> x1, Pallas kernels: none -> 51.8 us  [body(): pl.pallas_call(hand_over, out_shape=tuple((jax.ShapeDtypeStruct(x.shape,...]
    unnamed x20 -> x0, local copies, waits for them, and re-layouts: 10.2 us -> none
where the time goes in v1:
time: 90.4 us; the launch traced here: 90.2 us
  Pallas kernels  89.6 us (99%)
    pallas_call x1, Pallas kernels, body(): pl.pallas_call(hand_over, out_shape=tuple((jax.ShapeDtypeStruct(x.shape,...  51.8 us
    pallas_call x1, Pallas kernels, body(): pl.pallas_call(functools.partial(kernel, (n_rows, n_samp)), out_shape=(ja...  37.8 us

profile of v1, /device:TPU:9, one launch (start us, length us, event | category | flops | bytes accessed | tf_op | source)
XLA Modules:
  0.0 90.2 jit_solution(3144597649971814976)
XLA Ops:
  0.6 37.8 %shard_map.111 = (f32[64,1536]{1,0:T(8,128)}, f32[6,8,4096]{2,1,0:T(8,128)}, f32[3,64,128]{2,1,0:T(8,128)}, f32[3,8,4096]{2,1,0:T(8,128)}) custom-call(s32[6,8]{1,0:T(8,128)} %far_in.1, s32[6]{0:T(128)} %count_in.1, s32[3,8]{1,0:T(4,128)} %coarse_far_in.1, s32[3]{0:T(128)} %coarse_count_in.1, f32[64,256]{1,0:T(8,128)} %test_in.1, f32[64,256]{1,0:T(8,128)} %test_coarse_in.1, ...), custom_call_target="tpu_custom_call" | custom-call | flops 1000000000 | bytes 5000000 | tf_op jit(solution)/shard_map/pallas_call | solution.py:413
  38.4 51.8 %shard_map.112 = (f32[64,1536]{1,0:T(8,128)}, f32[6,8,4096]{2,1,0:T(8,128)}, f32[3,64,128]{2,1,0:T(8,128)}, f32[3,8,4096]{2,1,0:T(8,128)}) custom-call(f32[64,1536]{1,0:T(8,128)} %get-tuple-element.8.refs_0_, f32[6,8,4096]{2,1,0:T(8,128)} %get-tuple-element.9.refs_1_, f32[3,64,128]{2,1,0:T(8,128)} %get-tuple-element.10.refs_2_, ...), custom_call_target="tpu_custom_call" | custom-call | tf_op jit(solution)/shard_map/pallas_call | solution.py:458

commit v2 on v1

--- a/solution.py
+++ b/solution.py
@@ -390,14 +390,6 @@
         when(reaches(s), lambda s=s: coarse(s).wait_send())
 
 
-def hand_over(*refs):
-    copies = [pltpu.make_async_copy(refs[i], refs[4 + i], refs[8].at[i]) for i in range(4)]
-    for copy in copies:
-        copy.start()
-    for copy in copies:
-        copy.wait()
-
-
 def solution(mesh):
     n_rows, n_samp = mesh.shape["rows"], mesh.shape["samp"]
 
@@ -410,7 +402,7 @@
         vmem = pl.BlockSpec(memory_space=pltpu.VMEM)
         hbm = pl.BlockSpec(memory_space=pltpu.HBM)
         blocks = (n_samp, local, width)
-        made = pl.pallas_call(
+        return pl.pallas_call(
             functools.partial(kernel, (n_rows, n_samp)),
             out_shape=(
                 jax.ShapeDtypeStruct((rank, width), F32),
@@ -455,14 +447,6 @@
                 flops=10**9, bytes_accessed=5 * 10**6, transcendentals=0
             ),
         )(leaf_far, leaf_count, parent_far, parent_count, test_leaf, test_parent, sketch, probes)
-        return pl.pallas_call(
-            hand_over,
-            out_shape=tuple(jax.ShapeDtypeStruct(x.shape, x.dtype) for x in made),
-            in_specs=[hbm] * 4,
-            out_specs=(hbm,) * 4,
-            scratch_shapes=[pltpu.SemaphoreType.DMA((4,))],
-            compiler_params=pltpu.CompilerParams(vmem_limit_bytes=62 * 1024 * 1024),
-        )(*made)
 
     return jax.shard_map(
         body,

time: 90.4 us -> 43.9 us (0.49)
  Pallas kernels: 89.6 us -> 37.8 us
  local copies, waits for them, and re-layouts: 0 us -> 5.28 us
    pallas_call x1 -> x0, Pallas kernels: 51.8 us -> none  [body(): pl.pallas_call(hand_over, out_shape=tuple((jax.ShapeDtypeStruct(x.shape,...]
    unnamed x0 -> x8, local copies, waits for them, and re-layouts: none -> 5.28 us
where the time goes in v2:
time: 43.9 us; the launch traced here: 43.7 us
  Pallas kernels  37.8 us (86%)
  local copies, waits for them, and re-layouts  5.28 us (12%)
  between operations  0.66 us (2%)
    pallas_call x1, Pallas kernels, body(): pl.pallas_call(functools.partial(kernel, (n_rows, n_samp)), out_shape=(ja...  37.8 us
    unnamed x8, local copies, waits for them, and re-layouts  5.28 us

profile of v2, /device:TPU:9, one launch (start us, length us, event | category | flops | bytes accessed | tf_op | source)
XLA Modules:
  0.0 43.7 jit_solution(16096620112413697354)
XLA Ops:
  0.6 37.8 %shard_map.111 = (f32[64,1536]{1,0:T(8,128)}, f32[6,8,4096]{2,1,0:T(8,128)}, f32[3,64,128]{2,1,0:T(8,128)}, f32[3,8,4096]{2,1,0:T(8,128)}) custom-call(s32[6,8]{1,0:T(8,128)} %far_in.1, s32[6]{0:T(128)} %count_in.1, s32[3,8]{1,0:T(4,128)} %coarse_far_in.1, s32[3]{0:T(128)} %coarse_count_in.1, f32[64,256]{1,0:T(8,128)} %test_in.1, f32[64,256]{1,0:T(8,128)} %test_coarse_in.1, ...), custom_call_target="tpu_custom_call" | custom-call | flops 1000000000 | bytes 5000000 | tf_op jit(solution)/shard_map/pallas_call | solution.py:405
  38.4 0.0 copy-start.1
  38.4 0.0 copy-start
  38.4 1.8 %copy.16 = f32[64,1536]{1,0:T(8,128)} copy(f32[64,1536]{1,0:T(8,128)} %get-tuple-element.8) | data formatting | bytes 786432
  40.3 2.1 %copy.17 = f32[6,8,4096]{2,1,0:T(8,128)} copy(f32[6,8,4096]{2,1,0:T(8,128)} %get-tuple-element.9) | data formatting | bytes 1572864
  42.3 0.0 copy-done.1
  42.3 0.6 %copy.18 = f32[3,64,128]{2,1,0:T(8,128)} copy(f32[3,64,128]{2,1,0:T(8,128)S(1)} %copy-done.1) | data formatting | bytes 196608
  43.0 0.0 copy-done
  43.0 0.7 %copy.19 = f32[3,8,4096]{2,1,0:T(8,128)} copy(f32[3,8,4096]{2,1,0:T(8,128)S(1)} %copy-done) | data formatting | bytes 786432
Async XLA Ops:
  38.4 3.9 %copy-start.1 = (f32[3,64,128]{2,1,0:T(8,128)S(1)}, f32[3,64,128]{2,1,0:T(8,128)}, u32[]{:S(2)}) copy-start(f32[3,64,128]{2,1,0:T(8,128)} %get-tuple-element.10) | copy-start | bytes 294916
  38.4 4.5 %copy-start = (f32[3,8,4096]{2,1,0:T(8,128)S(1)}, f32[3,8,4096]{2,1,0:T(8,128)}, u32[]{:S(2)}) copy-start(f32[3,8,4096]{2,1,0:T(8,128)} %get-tuple-element.11) | copy-start | bytes 1179652
